TPU v7x, 256 devices: a whole 4x4x8 slice. The times are simulated.
256 devices in a mesh: dp: 8 (over z_lo, core), seq: 32 (over y, x, z_hi).
Axes of the slice: x: 4, y: 4, z: 8 (z_hi: 2, z_lo: 4; z = z_hi * 4 + z_lo), core: 2. Of those that a mesh axis runs over, the one named last changes fastest.
Arguments:
- first_input: bfloat16 [8, 16384, 128], P('dp', 'seq'), may hold values from -6 to 6
- value_input: bfloat16 [8, 16384, 128], P('dp', 'seq'), may hold values from -6 to 6
- gate_input: bfloat16 [8, 16384, 128], P('dp', 'seq'), may hold values from -6 to 6
- cotangent: bfloat16 [8, 16384, 128], P('dp', 'seq'), may hold values from -6 to 6
- filter_taps: float32 [16384, 128], P('seq'), may hold values from -4 to 4
- skip_weight: float32 [128], replicated, may hold values from -4 to 4
Outputs:
- layer_output: bfloat16 [8, 16384, 128], P('dp', 'seq')
- filter_grad: float32 [16384, 128], P('seq')
All inputs are finite; a program needn't handle non-finite values.
Results may differ from a plain program's by a relative error of at most 0.001.
Values sent between devices are 32-bit elements; how exact they have to be, the bound alone decides.
A program may use at most 64 MiB of HBM per device.

v0:
```python
import functools
import math
import jax
import jax.numpy as jnp
from jax import lax
from jax.sharding import PartitionSpec as P


def angles(numer, period):
    return 2.0 * math.pi / period * (numer % period).astype(jnp.float32)


def rotate(real_part, imag_part, phase, direction):
    cosine = jnp.cos(phase)
    sine = direction * jnp.sin(phase)
    return (real_part * cosine - imag_part * sine, real_part * sine + imag_part * cosine)


def local_transform(real_part, imag_part, direction):
    count, length = real_part.shape
    outer = 1 << (length.bit_length() - 1) // 2
    inner = length // outer
    real_cube = real_part.reshape(count, outer, inner)
    imag_cube = imag_part.reshape(count, outer, inner)
    outer_idx = lax.iota(jnp.int32, outer)
    inner_idx = lax.iota(jnp.int32, inner)
    first_phase = angles(outer_idx[:, None] * outer_idx[None, :], outer)
    first_cos = jnp.cos(first_phase)
    first_sin = direction * jnp.sin(first_phase)
    mix = functools.partial(
        jnp.einsum, precision=lax.Precision.HIGHEST, preferred_element_type=jnp.float32
    )
    section_real = mix("kp,cpq->ckq", first_cos, real_cube) - mix(
        "kp,cpq->ckq", first_sin, imag_cube
    )
    section_imag = mix("kp,cpq->ckq", first_cos, imag_cube) + mix(
        "kp,cpq->ckq", first_sin, real_cube
    )
    twiddle = angles(outer_idx[:, None] * inner_idx[None, :], length)
    section_real, section_imag = rotate(section_real, section_imag, twiddle, direction)
    second_phase = angles(inner_idx[:, None] * inner_idx[None, :], inner)
    second_cos = jnp.cos(second_phase)
    second_sin = direction * jnp.sin(second_phase)
    final_real = mix("ckq,jq->ckj", section_real, second_cos) - mix(
        "ckq,jq->ckj", section_imag, second_sin
    )
    final_imag = mix("ckq,jq->ckj", section_imag, second_cos) + mix(
        "ckq,jq->ckj", section_real, second_sin
    )
    final_real = jnp.transpose(final_real, (0, 2, 1)).reshape(count, length)
    final_imag = jnp.transpose(final_imag, (0, 2, 1)).reshape(count, length)
    return (final_real, final_imag)


def channel_layout(gated, weighted, filter_taps, gate_input, skip_weight):
    batch_local = gated.shape[0]
    moved_gated, moved_weighted, moved_taps = (
        lax.all_to_all(gated, "seq", split_axis=2, concat_axis=1, tiled=True),
        lax.all_to_all(weighted, "seq", split_axis=2, concat_axis=1, tiled=True),
        lax.all_to_all(filter_taps[None], "seq", split_axis=2, concat_axis=1, tiled=True),
    )
    length = moved_gated.shape[1]
    narrow = moved_gated.shape[2]
    spread = batch_local * narrow
    gated_rows = jnp.transpose(moved_gated, (0, 2, 1)).reshape(spread, length)
    weighted_rows = jnp.transpose(moved_weighted, (0, 2, 1)).reshape(spread, length)
    taps_rows = jnp.transpose(moved_taps[0], (1, 0))
    rows_all = jnp.concatenate([gated_rows, taps_rows, weighted_rows], axis=0)
    count = rows_all.shape[0]
    twist = angles(lax.iota(jnp.int32, length), 2 * length)[None, :]
    cos_twist = jnp.cos(twist)
    sin_twist = jnp.sin(twist)
    real_in = jnp.concatenate([rows_all, rows_all * cos_twist], axis=0)
    imag_in = jnp.concatenate([jnp.zeros_like(rows_all), -rows_all * sin_twist], axis=0)
    spec_real, spec_imag = local_transform(real_in, imag_in, -1.0)
    spec_real = spec_real.reshape(2, count, length)
    spec_imag = spec_imag.reshape(2, count, length)
    gated_real = spec_real[:, :spread].reshape(2, batch_local, narrow, length)
    gated_imag = spec_imag[:, :spread].reshape(2, batch_local, narrow, length)
    taps_real = spec_real[:, spread : spread + narrow][:, None]
    taps_imag = spec_imag[:, spread : spread + narrow][:, None]
    source_real = spec_real[:, spread + narrow :].reshape(2, batch_local, narrow, length)
    source_imag = spec_imag[:, spread + narrow :].reshape(2, batch_local, narrow, length)
    conv_real = (gated_real * taps_real - gated_imag * taps_imag).reshape(2, spread, length)
    conv_imag = (gated_real * taps_imag + gated_imag * taps_real).reshape(2, spread, length)
    grad_real = jnp.sum(source_real * gated_real + source_imag * gated_imag, axis=1)
    grad_imag = jnp.sum(source_imag * gated_real - source_real * gated_imag, axis=1)
    back_real = jnp.concatenate([conv_real, grad_real], axis=1).reshape(-1, length)
    back_imag = jnp.concatenate([conv_imag, grad_imag], axis=1).reshape(-1, length)
    back_real, back_imag = local_transform(back_real, back_imag, 1.0)
    back_real = back_real.reshape(2, -1, length)
    back_imag = back_imag.reshape(2, -1, length)
    joined = (back_real[0] + back_real[1] * cos_twist - back_imag[1] * sin_twist) / (2.0 * length)
    convolved = jnp.transpose(joined[:spread].reshape(batch_local, narrow, length), (0, 2, 1))
    grad_time = lax.psum(jnp.transpose(joined[spread:], (1, 0)), "dp")
    convolved, grad_back = (
        lax.all_to_all(convolved, "seq", split_axis=1, concat_axis=2, tiled=True),
        lax.all_to_all(grad_time[None], "seq", split_axis=1, concat_axis=2, tiled=True),
    )
    layer_output = (gate_input.astype(jnp.float32) * (convolved + skip_weight * gated)).astype(
        jnp.bfloat16
    )
    scale = 1.0 / math.sqrt(batch_local * lax.axis_size("dp") * length)
    return (layer_output, grad_back[0] * scale)


def shards(first_input, value_input, gate_input, cotangent, filter_taps, skip_weight):
    gated = first_input.astype(jnp.float32) * value_input.astype(jnp.float32)
    weighted = cotangent.astype(jnp.float32) * gate_input.astype(jnp.float32)
    return channel_layout(gated, weighted, filter_taps, gate_input, skip_weight)


def solution(mesh):
    placed = (
        P("dp", "seq", None),
        P("dp", "seq", None),
        P("dp", "seq", None),
        P("dp", "seq", None),
        P("seq", None),
        P(),
    )
    return jax.shard_map(
        shards,
        mesh=mesh,
        in_specs=placed,
        out_specs=(P("dp", "seq", None), P("seq", None)),
        check_vma=False,
    )
```

profile of v0, /device:TPU:2, one launch (start us, length us, event | category | flops | bytes accessed | tf_op | source)
XLA Modules:
  0.0 486.5 jit_solution(10669566144408117033)
XLA Ops:
  9.1 14.2 %all-to-all-start.2 = ((f32[1,512,128]{1,0,2:T(1,128)}), f32[1,512,128]{1,0,2:T(1,128)S(1)}, u32[]{:S(2)}, u32[]{:S(2)}) async-start(f32[1,512,128]{1,0,2:T(1,128)} %copy.157), calls=%async_computation.2 | async-start | bytes 524288 | tf_op jit(solution)/shard_map/all_to_all | solution.py:59
  24.2 11.4 %all-to-all-done.2 = f32[1,512,128]{1,0,2:T(1,128)S(1)} async-done(((f32[1,512,128]{1,0,2:T(1,128)}), f32[1,512,128]{1,0,2:T(1,128)S(1)}, u32[]{:S(2)}, u32[]{:S(2)}) %all-to-all-start.2) | async-done | bytes 262176 | tf_op jit(solution)/shard_map/all_to_all | solution.py:59
  35.6 5.0 %all-to-all-start.1 = ((f32[1,512,128]{1,0,2:T(1,128)}), f32[1,512,128]{1,0,2:T(1,128)S(1)}, u32[]{:S(2)}, u32[]{:S(2)}) async-start(f32[1,512,128]{1,0,2:T(1,128)} %copy.211), calls=%async_computation.1 | async-start | bytes 524288 | tf_op jit(solution)/shard_map/all_to_all | solution.py:60
  42.2 10.6 %all-to-all-done.1 = f32[1,512,128]{1,0,2:T(1,128)S(1)} async-done(((f32[1,512,128]{1,0,2:T(1,128)}), f32[1,512,128]{1,0,2:T(1,128)S(1)}, u32[]{:S(2)}, u32[]{:S(2)}) %all-to-all-start.1) | async-done | bytes 262176 | tf_op jit(solution)/shard_map/all_to_all | solution.py:60
  52.9 6.1 %all-to-all-start = ((f32[1,512,128]{1,0,2:T(1,128)}), f32[1,512,128]{1,0,2:T(1,128)S(1)}, u32[]{:S(2)}, u32[]{:S(2)}) async-start(f32[1,512,128]{1,0,2:T(1,128)} %copy.153), calls=%async_computation | async-start | bytes 524288 | tf_op jit(solution)/shard_map/all_to_all | solution.py:58
  62.3 8.7 %all-to-all-done = f32[1,512,128]{1,0,2:T(1,128)S(1)} async-done(((f32[1,512,128]{1,0,2:T(1,128)}), f32[1,512,128]{1,0,2:T(1,128)S(1)}, u32[]{:S(2)}, u32[]{:S(2)}) %all-to-all-start) | async-done | bytes 262176 | tf_op jit(solution)/shard_map/all_to_all | solution.py:58
  73.8 2.8 fusion.45
  76.6 2.8 convolution_subtract_fusion
  81.1 3.4 fusion.11
  84.5 4.0 fusion.15
  88.5 4.0 add_bitcast_fusion
  92.5 3.0 copy.175
  95.6 3.1 reshape_reshape.15
  98.6 5.4 %subtract_bitcast_fusion = f32[24,128,128]{1,2,0:T(8,128)} fusion(f32[24,128,128]{2,1,0:T(8,128)} %fusion.15, f32[24,128,128]{2,1,0:T(8,128)S(1)} %convolution_add_fusion, f32[24,128,128]{2,1,0:T(8,128)S(1)} %convolution_subtract_fusion, f32[128,128]{0,1:T(8,128)S(1)} %copy.169, f32[128,128]{0,1:T(8,128)S(1)} %copy.167), kind=kOutput, calls=%fused_computation.8 | convolution fusion | flops 605798400 | bytes 6422528 | tf_op jit(solution)/shard_map/ckq,jq->ckj/dot_general | solution.py:44
  104.0 3.2 copy.172
  107.2 3.2 reshape_reshape.14
  110.4 2.4 multiply_subtract_fusion.2
  123.5 2.2 fusion.17
  128.5 2.0 copy.188
  135.5 12.0 %copy.189 = f32[1,16384,4]{2,0,1:T(1,128)} copy(f32[1,16384,4]{1,2,0:T(4,128)S(1)} %get-tuple-element.17) | data formatting | bytes 524288 | tf_op jit(solution)/shard_map/transpose | solution.py:94
  148.0 74.5 %reduce = f32[16384,4]{1,0:T(8,128)} reduce(f32[16384,1,4]{2,1,0:T(1,128)} %bitcast.179, f32[]{:T(128)} %broadcast.236), dimensions={1}, to_apply=%bitcast.163.reduce_sub_computation | reduce | bytes 524292
  222.6 9.5 %reshape.143 = f32[32,1,2048]{2,1,0:T(1,128)} reshape(f32[16384,4]{1,0:T(8,128)} %reduce) | data formatting | bytes 524288
  232.0 5.9 %all-to-all-start.3 = ((f32[32,1,2048]{2,1,0:T(1,128)}), f32[32,1,2048]{2,1,0:T(1,128)S(1)}, u32[]{:S(2)}, u32[]{:S(2)}) async-start(f32[32,1,2048]{2,1,0:T(1,128)} %reshape.143), calls=%async_computation.3 | async-start | bytes 524288 | tf_op jit(solution)/shard_map/all_to_all | solution.py:97
  238.7 77.0 %all-reduce.3.cloned.1.call-done = f32[1,16384,4]{1,2,0:T(4,128)} async-done(((f32[1,16384,4]{1,2,0:T(4,128)}), f32[1,16384,4]{1,2,0:T(4,128)}) %all-reduce.3.cloned.1.call-update) | async-done | bytes 262160 | tf_op jit(solution)/shard_map/psum | solution.py:95
  315.7 14.8 %copy.193 = f32[1,16384,4]{2,0,1:T(1,128)} copy(f32[1,16384,4]{1,2,0:T(4,128)} %all-reduce.3.cloned.1.call-done) | data formatting | bytes 524288 | tf_op jit(solution)/shard_map/psum | solution.py:95
  330.6 74.5 %reduce.2 = f32[16384,4]{1,0:T(8,128)} reduce(f32[16384,1,4]{2,1,0:T(1,128)} %bitcast.180, f32[]{:T(128)} %broadcast.236), dimensions={1}, to_apply=%bitcast.165.reduce_sub_computation | reduce | bytes 524292
  405.1 9.1 %reshape.145 = f32[32,1,2048]{2,1,0:T(1,128)} reshape(f32[16384,4]{1,0:T(8,128)} %reduce.2) | data formatting | bytes 524288
  414.2 10.4 %all-to-all-start.4 = ((f32[32,1,2048]{2,1,0:T(1,128)}), f32[32,1,2048]{2,1,0:T(1,128)S(1)}, u32[]{:S(2)}, u32[]{:S(2)}) async-start(f32[32,1,2048]{2,1,0:T(1,128)} %reshape.145), calls=%async_computation.4 | async-start | bytes 524288 | tf_op jit(solution)/shard_map/all_to_all | solution.py:98
  425.9 14.8 %reshape.144 = f32[16384,1,4]{2,1,0:T(1,128)} reshape(f32[32,2048]{1,0:T(8,128)S(1)} %reduce.1) | data formatting | bytes 524288
  440.6 5.3 %copy.212 = f32[1,32,512,4]{2,1,3,0:T(8,128)S(1)} copy(f32[1,32,512,4]{3,2,1,0:T(8,128)} %bitcast.181) | data formatting | bytes 524288 | tf_op jit(solution)/shard_map/all_to_all | solution.py:97
  448.4 14.8 %reshape.146 = f32[16384,1,4]{2,1,0:T(1,128)} reshape(f32[32,2048]{1,0:T(8,128)S(1)} %reduce.3) | data formatting | bytes 524288
  463.2 15.0 %copy.194 = f32[1,16384,4]{1,2,0:T(4,128)S(1)} copy(f32[1,16384,4]{2,0,1:T(1,128)} %bitcast.182) | data formatting | bytes 524288 | tf_op jit(solution)/shard_map/all_to_all | solution.py:98
  (98 shorter events, 36.5 us)
Async XLA Ops:
  7.2 16.2 %copy-start.15 = (f32[512,128]{1,0:T(8,128)S(1)}, f32[512,128]{1,0:T(8,128)}, u32[]{:S(2)}) copy-start(f32[512,128]{1,0:T(8,128)} %param.10) | copy-start | bytes 786436
  7.2 33.4 %copy-start.10 = (bf16[1,512,128]{2,1,0:T(8,128)(2,1)S(1)}, bf16[1,512,128]{2,1,0:T(8,128)(2,1)}, u32[]{:S(2)}) copy-start(bf16[1,512,128]{2,1,0:T(8,128)(2,1)} %param.7) | copy-start | bytes 393220
  7.2 33.4 %copy-start.12 = (bf16[1,512,128]{2,1,0:T(8,128)(2,1)S(1)}, bf16[1,512,128]{2,1,0:T(8,128)(2,1)}, u32[]{:S(2)}) copy-start(bf16[1,512,128]{2,1,0:T(8,128)(2,1)} %param.6) | copy-start | bytes 393220
  9.1 26.5 %all-to-all-start.2 = ((f32[1,512,128]{1,0,2:T(1,128)}), f32[1,512,128]{1,0,2:T(1,128)S(1)}, u32[]{:S(2)}, u32[]{:S(2)}) async-start(f32[1,512,128]{1,0,2:T(1,128)} %copy.157), calls=%async_computation.2 | async-start | bytes 524288 | tf_op jit(solution)/shard_map/all_to_all | solution.py:59
  35.6 17.3 %all-to-all-start.1 = ((f32[1,512,128]{1,0,2:T(1,128)}), f32[1,512,128]{1,0,2:T(1,128)S(1)}, u32[]{:S(2)}, u32[]{:S(2)}) async-start(f32[1,512,128]{1,0,2:T(1,128)} %copy.211), calls=%async_computation.1 | async-start | bytes 524288 | tf_op jit(solution)/shard_map/all_to_all | solution.py:60
  52.9 18.1 %all-to-all-start = ((f32[1,512,128]{1,0,2:T(1,128)}), f32[1,512,128]{1,0,2:T(1,128)S(1)}, u32[]{:S(2)}, u32[]{:S(2)}) async-start(f32[1,512,128]{1,0,2:T(1,128)} %copy.153), calls=%async_computation | async-start | bytes 524288 | tf_op jit(solution)/shard_map/all_to_all | solution.py:58
  60.5 10.9 %copy-start.7 = (f32[16384]{0:T(1024)}, f32[16384]{0:T(1024)S(1)}, u32[]{:S(2)}) copy-start(f32[16384]{0:T(1024)S(1)} %fusion.51) | copy-start | bytes 196612
  62.3 9.8 %copy-start.1 = (f32[4,128,128]{1,2,0:T(8,128)}, f32[4,128,128]{1,2,0:T(8,128)S(1)}, u32[]{:S(2)}) copy-start(f32[4,128,128]{1,2,0:T(8,128)S(1)} %copy.164) | copy-start | bytes 786436
  71.4 0.7 copy-start.3
  76.6 2.9 copy-start.2
  76.6 2.9 copy-start.4
  107.2 3.2 copy-start
  119.5 1.9 copy-start.6
  132.7 1.0 copy-start.5
  132.7 1.0 copy-start.8
  132.7 1.0 copy-start.14
  232.0 182.2 %all-to-all-start.3 = ((f32[32,1,2048]{2,1,0:T(1,128)}), f32[32,1,2048]{2,1,0:T(1,128)S(1)}, u32[]{:S(2)}, u32[]{:S(2)}) async-start(f32[32,1,2048]{2,1,0:T(1,128)} %reshape.143), calls=%async_computation.3 | async-start | bytes 524288 | tf_op jit(solution)/shard_map/all_to_all | solution.py:97
  238.0 77.8 %all-reduce.3.cloned.1.call-start = ((), (), s32[]{:S(2)}) async-start(), calls=%async_computation.5 | async-start | bytes 524288 | tf_op jit(solution)/shard_map/psum | solution.py:95
  414.2 33.0 %all-to-all-start.4 = ((f32[32,1,2048]{2,1,0:T(1,128)}), f32[32,1,2048]{2,1,0:T(1,128)S(1)}, u32[]{:S(2)}, u32[]{:S(2)}) async-start(f32[32,1,2048]{2,1,0:T(1,128)} %reshape.145), calls=%async_computation.4 | async-start | bytes 524288 | tf_op jit(solution)/shard_map/all_to_all | solution.py:98
  440.6 5.7 %copy-start.9 = (bf16[1,512,128]{2,1,0:T(8,128)(2,1)S(1)}, bf16[1,512,128]{2,1,0:T(8,128)(2,1)}, u32[]{:S(2)}) copy-start(bf16[1,512,128]{2,1,0:T(8,128)(2,1)} %param.8) | copy-start | bytes 393220
  440.6 5.7 %copy-start.11 = (bf16[1,512,128]{2,1,0:T(8,128)(2,1)S(1)}, bf16[1,512,128]{2,1,0:T(8,128)(2,1)}, u32[]{:S(2)}) copy-start(bf16[1,512,128]{2,1,0:T(8,128)(2,1)} %param.7) | copy-start | bytes 393220
  440.6 5.7 %copy-start.13 = (bf16[1,512,128]{2,1,0:T(8,128)(2,1)S(1)}, bf16[1,512,128]{2,1,0:T(8,128)(2,1)}, u32[]{:S(2)}) copy-start(bf16[1,512,128]{2,1,0:T(8,128)(2,1)} %param.6) | copy-start | bytes 393220
  440.6 5.7 %copy-start.16 = (f32[128]{0:T(128)S(1)}, f32[128]{0:T(128)}, u32[]{:S(2)}) copy-start(f32[128]{0:T(128)} %param.11) | copy-start | bytes 1540
Sparse Core Ops, SparseCore 0:
  242.0 73.7 all-reduce.2
where the time goes:
time: 491 us; the launch traced here: 486 us
  other arithmetic  160 us (33%)
  local copies, waits for them, and re-layouts  120 us (24%)
  waiting for transfers between devices  108 us (22%)
  starting transfers between devices  41.7 us (8%)
  matrix products  41.6 us (8%)
  between operations  14.9 us (3%)
    unnamed x3, other arithmetic  149 us
    psum x1, waiting for transfers between devices, channel_layout(): grad_time = lax.psum(jnp.transpose(joined[spread:], (1, 0)), 'dp')  77 us
    unnamed x49, local copies, waits for them, and re-layouts  51.3 us
    all_to_all x1, local copies, waits for them, and re-layouts, channel_layout(): lax.all_to_all(grad_time[None], 'seq', split_axis=1, concat_axis=2, tiled...  15 us
    psum x1, local copies, waits for them, and re-layouts, channel_layout(): grad_time = lax.psum(jnp.transpose(joined[spread:], (1, 0)), 'dp')  14.8 us
    all_to_all x1, starting transfers between devices, channel_layout(): lax.all_to_all(weighted, 'seq', split_axis=2, concat_axis=1, tiled=True)  14.2 us
    transpose x1, local copies, waits for them, and re-layouts, channel_layout(): jnp.transpose(joined[:spread].reshape(batch_local, narrow, length), (0, 2...  12 us
    all_to_all x1, waiting for transfers between devices, channel_layout(): lax.all_to_all(weighted, 'seq', split_axis=2, concat_axis=1, tiled=True)  11.4 us
  transfers between devices with their start and end apart: 6, of which 4 were waited for; matrix products, arithmetic and copies ran while one was open for 26% of the time, Pallas kernels for 0%

commit v1 on v0

--- a/solution.py
+++ b/solution.py
@@ -92,7 +92,8 @@
     back_imag = back_imag.reshape(2, -1, length)
     joined = (back_real[0] + back_real[1] * cos_twist - back_imag[1] * sin_twist) / (2.0 * length)
     convolved = jnp.transpose(joined[:spread].reshape(batch_local, narrow, length), (0, 2, 1))
-    grad_time = lax.psum(jnp.transpose(joined[spread:], (1, 0)), "dp")
+    values = jnp.transpose(joined[spread:], (1, 0))
+    grad_time = lax.all_gather(values, "dp").sum(axis=0)
     convolved, grad_back = (
         lax.all_to_all(convolved, "seq", split_axis=1, concat_axis=2, tiled=True),
         lax.all_to_all(grad_time[None], "seq", split_axis=1, concat_axis=2, tiled=True),

time: 491 us -> 417 us (0.85)
  waiting for transfers between devices: 108 us -> 30.7 us
    psum x1 -> x0, waiting for transfers between devices: 77 us -> none  [channel_layout(): grad_time = lax.psum(jnp.transpose(joined[spread:], (1, 0)), 'dp')]
    psum x1 -> x0, local copies, waits for them, and re-layouts: 14.8 us -> none  [channel_layout(): grad_time = lax.psum(jnp.transpose(joined[spread:], (1, 0)), 'dp')]
    broadcast_in_dim x1, local copies, waits for them, and re-layouts: 0.78 us -> 12.1 us  [channel_layout(): grad_time[None]]
  transfers between devices with their start and end apart: 6 -> 6, of which waited for: 4 -> 3; matrix products, arithmetic and copies ran while one was open for 26% -> 54% of each run, Pallas kernels for 0% -> 0%
where the time goes in v1:
time: 417 us; the launch traced here: 412 us
  other arithmetic  163 us (39%)
  local copies, waits for them, and re-layouts  117 us (28%)
  starting transfers between devices  44.3 us (11%)
  matrix products  41.6 us (10%)
  waiting for transfers between devices  30.7 us (7%)
  between operations  14.9 us (4%)
    unnamed x3, other arithmetic  150 us
    unnamed x49, local copies, waits for them, and re-layouts  50.9 us
    all_to_all x1, local copies, waits for them, and re-layouts, channel_layout(): lax.all_to_all(grad_time[None], 'seq', split_axis=1, concat_axis=2, tiled...  15 us
    all_to_all x1, starting transfers between devices, channel_layout(): lax.all_to_all(weighted, 'seq', split_axis=2, concat_axis=1, tiled=True)  14.2 us
    all_to_all x1, starting transfers between devices, channel_layout(): lax.all_to_all(grad_time[None], 'seq', split_axis=1, concat_axis=2, tiled...  12.5 us
    transpose x1, local copies, waits for them, and re-layouts, channel_layout(): jnp.transpose(joined[:spread].reshape(batch_local, narrow, length), (0, 2...  12.1 us
    broadcast_in_dim x1, local copies, waits for them, and re-layouts, channel_layout(): grad_time[None]  12.1 us
    all_to_all x1, waiting for transfers between devices, channel_layout(): lax.all_to_all(weighted, 'seq', split_axis=2, concat_axis=1, tiled=True)  11.4 us
  transfers between devices with their start and end apart: 6, of which 3 were waited for; matrix products, arithmetic and copies ran while one was open for 54% of the time, Pallas kernels for 0%

profile of v1, /device:TPU:2, one launch (start us, length us, event | category | flops | bytes accessed | tf_op | source)
XLA Modules:
  0.0 411.7 jit_solution(8138178048912847619)
XLA Ops:
  9.1 14.2 %all-to-all-start.2 = ((f32[1,512,128]{1,0,2:T(1,128)}), f32[1,512,128]{1,0,2:T(1,128)S(1)}, u32[]{:S(2)}, u32[]{:S(2)}) async-start(f32[1,512,128]{1,0,2:T(1,128)} %copy.202), calls=%async_computation.2 | async-start | bytes 524288 | tf_op jit(solution)/shard_map/all_to_all | solution.py:59
  24.2 11.4 %all-to-all-done.2 = f32[1,512,128]{1,0,2:T(1,128)S(1)} async-done(((f32[1,512,128]{1,0,2:T(1,128)}), f32[1,512,128]{1,0,2:T(1,128)S(1)}, u32[]{:S(2)}, u32[]{:S(2)}) %all-to-all-start.2) | async-done | bytes 262176 | tf_op jit(solution)/shard_map/all_to_all | solution.py:59
  35.6 5.0 %all-to-all-start.1 = ((f32[1,512,128]{1,0,2:T(1,128)}), f32[1,512,128]{1,0,2:T(1,128)S(1)}, u32[]{:S(2)}, u32[]{:S(2)}) async-start(f32[1,512,128]{1,0,2:T(1,128)} %copy.256), calls=%async_computation.1 | async-start | bytes 524288 | tf_op jit(solution)/shard_map/all_to_all | solution.py:60
  42.2 10.6 %all-to-all-done.1 = f32[1,512,128]{1,0,2:T(1,128)S(1)} async-done(((f32[1,512,128]{1,0,2:T(1,128)}), f32[1,512,128]{1,0,2:T(1,128)S(1)}, u32[]{:S(2)}, u32[]{:S(2)}) %all-to-all-start.1) | async-done | bytes 262176 | tf_op jit(solution)/shard_map/all_to_all | solution.py:60
  52.9 5.8 %all-to-all-start = ((f32[1,512,128]{1,0,2:T(1,128)}), f32[1,512,128]{1,0,2:T(1,128)S(1)}, u32[]{:S(2)}, u32[]{:S(2)}) async-start(f32[1,512,128]{1,0,2:T(1,128)} %copy.198), calls=%async_computation | async-start | bytes 524288 | tf_op jit(solution)/shard_map/all_to_all | solution.py:58
  62.3 8.6 %all-to-all-done = f32[1,512,128]{1,0,2:T(1,128)S(1)} async-done(((f32[1,512,128]{1,0,2:T(1,128)}), f32[1,512,128]{1,0,2:T(1,128)S(1)}, u32[]{:S(2)}, u32[]{:S(2)}) %all-to-all-start) | async-done | bytes 262176 | tf_op jit(solution)/shard_map/all_to_all | solution.py:58
  73.8 2.8 fusion.45
  76.6 2.8 convolution_subtract_fusion
  81.1 3.4 fusion.11
  84.5 4.0 fusion.15
  88.5 4.0 add_bitcast_fusion
  92.5 3.0 copy.220
  95.6 3.1 reshape_reshape.15
  98.6 5.4 %subtract_bitcast_fusion = f32[24,128,128]{1,2,0:T(8,128)} fusion(f32[24,128,128]{2,1,0:T(8,128)} %fusion.15, f32[24,128,128]{2,1,0:T(8,128)S(1)} %convolution_add_fusion, f32[24,128,128]{2,1,0:T(8,128)S(1)} %convolution_subtract_fusion, f32[128,128]{0,1:T(8,128)S(1)} %copy.214, f32[128,128]{0,1:T(8,128)S(1)} %copy.212), kind=kOutput, calls=%fused_computation.9 | convolution fusion | flops 605798400 | bytes 6422528 | tf_op jit(solution)/shard_map/ckq,jq->ckj/dot_general | solution.py:44
  104.0 3.2 copy.217
  107.2 3.2 reshape_reshape.14
  110.4 2.4 multiply_subtract_fusion.2
  123.5 2.2 fusion.17
  128.5 2.0 copy.233
  135.5 12.1 %copy.234 = f32[1,16384,4]{2,0,1:T(1,128)} copy(f32[1,16384,4]{1,2,0:T(4,128)S(1)} %get-tuple-element.19) | data formatting | bytes 524288 | tf_op jit(solution)/shard_map/transpose | solution.py:94
  148.2 74.5 %reduce = f32[16384,4]{1,0:T(8,128)} reduce(f32[16384,1,4]{2,1,0:T(1,128)} %bitcast.183, f32[]{:T(128)} %broadcast.236), dimensions={1}, to_apply=%bitcast.167.reduce_sub_computation | reduce | bytes 524292
  222.7 9.1 %reshape.144 = f32[32,1,2048]{2,1,0:T(1,128)} reshape(f32[16384,4]{1,0:T(8,128)} %reduce) | data formatting | bytes 524288
  231.8 6.4 %all-to-all-start.3 = ((f32[32,1,2048]{2,1,0:T(1,128)}), f32[32,1,2048]{2,1,0:T(1,128)S(1)}, u32[]{:S(2)}, u32[]{:S(2)}) async-start(f32[32,1,2048]{2,1,0:T(1,128)} %reshape.144), calls=%async_computation.3 | async-start | bytes 524288 | tf_op jit(solution)/shard_map/all_to_all | solution.py:98
  238.2 3.3 bitcast_reduce_fusion
  241.5 12.1 %copy.238 = f32[1,16384,4]{2,0,1:T(1,128)} copy(f32[1,16384,4]{1,2,0:T(4,128)S(1)} %bitcast.203) | data formatting | bytes 524288 | tf_op jit(solution)/shard_map/broadcast_in_dim | solution.py:99
  253.6 74.5 %reduce.2 = f32[16384,4]{1,0:T(8,128)} reduce(f32[16384,1,4]{2,1,0:T(1,128)} %bitcast.184, f32[]{:T(128)} %broadcast.236), dimensions={1}, to_apply=%bitcast.169.reduce_sub_computation | reduce | bytes 524292
  328.2 9.1 %reshape.146 = f32[32,1,2048]{2,1,0:T(1,128)} reshape(f32[16384,4]{1,0:T(8,128)} %reduce.2) | data formatting | bytes 524288
  337.2 12.5 %all-to-all-start.4 = ((f32[32,1,2048]{2,1,0:T(1,128)}), f32[32,1,2048]{2,1,0:T(1,128)S(1)}, u32[]{:S(2)}, u32[]{:S(2)}) async-start(f32[32,1,2048]{2,1,0:T(1,128)} %reshape.146), calls=%async_computation.4 | async-start | bytes 524288 | tf_op jit(solution)/shard_map/all_to_all | solution.py:99
  351.0 14.8 %reshape.145 = f32[16384,1,4]{2,1,0:T(1,128)} reshape(f32[32,2048]{1,0:T(8,128)S(1)} %reduce.1) | data formatting | bytes 524288
  365.8 5.3 %copy.257 = f32[1,32,512,4]{2,1,3,0:T(8,128)S(1)} copy(f32[1,32,512,4]{3,2,1,0:T(8,128)} %bitcast.185) | data formatting | bytes 524288 | tf_op jit(solution)/shard_map/all_to_all | solution.py:98
  373.6 14.8 %reshape.147 = f32[16384,1,4]{2,1,0:T(1,128)} reshape(f32[32,2048]{1,0:T(8,128)S(1)} %reduce.3) | data formatting | bytes 524288
  388.4 15.0 %copy.239 = f32[1,16384,4]{1,2,0:T(4,128)S(1)} copy(f32[1,16384,4]{2,0,1:T(1,128)} %bitcast.186) | data formatting | bytes 524288 | tf_op jit(solution)/shard_map/all_to_all | solution.py:99
  (99 shorter events, 36.2 us)
Async XLA Ops:
  7.2 16.2 %copy-start.15 = (f32[512,128]{1,0:T(8,128)S(1)}, f32[512,128]{1,0:T(8,128)}, u32[]{:S(2)}) copy-start(f32[512,128]{1,0:T(8,128)} %param.10) | copy-start | bytes 786436
  7.2 33.4 %copy-start.10 = (bf16[1,512,128]{2,1,0:T(8,128)(2,1)S(1)}, bf16[1,512,128]{2,1,0:T(8,128)(2,1)}, u32[]{:S(2)}) copy-start(bf16[1,512,128]{2,1,0:T(8,128)(2,1)} %param.7) | copy-start | bytes 393220
  7.2 33.4 %copy-start.12 = (bf16[1,512,128]{2,1,0:T(8,128)(2,1)S(1)}, bf16[1,512,128]{2,1,0:T(8,128)(2,1)}, u32[]{:S(2)}) copy-start(bf16[1,512,128]{2,1,0:T(8,128)(2,1)} %param.6) | copy-start | bytes 393220
  9.1 26.5 %all-to-all-start.2 = ((f32[1,512,128]{1,0,2:T(1,128)}), f32[1,512,128]{1,0,2:T(1,128)S(1)}, u32[]{:S(2)}, u32[]{:S(2)}) async-start(f32[1,512,128]{1,0,2:T(1,128)} %copy.202), calls=%async_computation.2 | async-start | bytes 524288 | tf_op jit(solution)/shard_map/all_to_all | solution.py:59
  35.6 17.3 %all-to-all-start.1 = ((f32[1,512,128]{1,0,2:T(1,128)}), f32[1,512,128]{1,0,2:T(1,128)S(1)}, u32[]{:S(2)}, u32[]{:S(2)}) async-start(f32[1,512,128]{1,0,2:T(1,128)} %copy.256), calls=%async_computation.1 | async-start | bytes 524288 | tf_op jit(solution)/shard_map/all_to_all | solution.py:60
  52.9 18.1 %all-to-all-start = ((f32[1,512,128]{1,0,2:T(1,128)}), f32[1,512,128]{1,0,2:T(1,128)S(1)}, u32[]{:S(2)}, u32[]{:S(2)}) async-start(f32[1,512,128]{1,0,2:T(1,128)} %copy.198), calls=%async_computation | async-start | bytes 524288 | tf_op jit(solution)/shard_map/all_to_all | solution.py:58
  58.7 179.5 %all-gather.3.cloned.1.call-start = ((), (), s32[]{:S(2)}) async-start(), calls=%async_computation.5 | async-start | bytes 2359296 | tf_op jit(solution)/shard_map/all_gather | solution.py:96
  60.6 10.8 %copy-start.7 = (f32[16384]{0:T(1024)}, f32[16384]{0:T(1024)S(1)}, u32[]{:S(2)}) copy-start(f32[16384]{0:T(1024)S(1)} %fusion.51) | copy-start | bytes 196612
  62.3 9.8 %copy-start.1 = (f32[4,128,128]{1,2,0:T(8,128)}, f32[4,128,128]{1,2,0:T(8,128)S(1)}, u32[]{:S(2)}) copy-start(f32[4,128,128]{1,2,0:T(8,128)S(1)} %copy.209) | copy-start | bytes 786436
  71.4 0.7 copy-start.3
  76.6 2.9 copy-start.2
  76.6 2.9 copy-start.4
  107.2 3.2 copy-start
  119.5 1.9 copy-start.6
  132.7 1.0 copy-start.5
  132.7 1.0 copy-start.8
  132.7 1.0 copy-start.14
  231.8 105.5 %all-to-all-start.3 = ((f32[32,1,2048]{2,1,0:T(1,128)}), f32[32,1,2048]{2,1,0:T(1,128)S(1)}, u32[]{:S(2)}, u32[]{:S(2)}) async-start(f32[32,1,2048]{2,1,0:T(1,128)} %reshape.144), calls=%async_computation.3 | async-start | bytes 524288 | tf_op jit(solution)/shard_map/all_to_all | solution.py:98
  337.2 35.1 %all-to-all-start.4 = ((f32[32,1,2048]{2,1,0:T(1,128)}), f32[32,1,2048]{2,1,0:T(1,128)S(1)}, u32[]{:S(2)}, u32[]{:S(2)}) async-start(f32[32,1,2048]{2,1,0:T(1,128)} %reshape.146), calls=%async_computation.4 | async-start | bytes 524288 | tf_op jit(solution)/shard_map/all_to_all | solution.py:99
  365.8 5.7 %copy-start.9 = (bf16[1,512,128]{2,1,0:T(8,128)(2,1)S(1)}, bf16[1,512,128]{2,1,0:T(8,128)(2,1)}, u32[]{:S(2)}) copy-start(bf16[1,512,128]{2,1,0:T(8,128)(2,1)} %param.8) | copy-start | bytes 393220
  365.8 5.7 %copy-start.11 = (bf16[1,512,128]{2,1,0:T(8,128)(2,1)S(1)}, bf16[1,512,128]{2,1,0:T(8,128)(2,1)}, u32[]{:S(2)}) copy-start(bf16[1,512,128]{2,1,0:T(8,128)(2,1)} %param.7) | copy-start | bytes 393220
  365.8 5.7 %copy-start.13 = (bf16[1,512,128]{2,1,0:T(8,128)(2,1)S(1)}, bf16[1,512,128]{2,1,0:T(8,128)(2,1)}, u32[]{:S(2)}) copy-start(bf16[1,512,128]{2,1,0:T(8,128)(2,1)} %param.6) | copy-start | bytes 393220
  365.8 5.7 %copy-start.16 = (f32[128]{0:T(128)S(1)}, f32[128]{0:T(128)}, u32[]{:S(2)}) copy-start(f32[128]{0:T(128)} %param.11) | copy-start | bytes 1540
Sparse Core Ops, SparseCore 0:
  135.6 36.9 all-gather.2
